TPU v7x, 32 devices: a whole 2x2x4 slice. The times are simulated.
32 devices in a mesh: row: 8 (over z, x), col: 4 (over y, core).
Axes of the slice: x: 2, y: 2, z: 4, core: 2. Of those that a mesh axis runs over, the one named last changes fastest.
Arguments:
- amplitudes: float32 [3072, 4, 2048], P(('row', 'col')), may hold values from -6 to 6
- integrals: float32 [2048, 4, 2048], P('row', None, 'col'), may hold values from -0.0625 to 0.0625
Outputs:
- ladder: float32 [3072, 2048], P('col', 'row')
All inputs are finite; a program needn't handle non-finite values.
Results may differ from a plain program's by a relative error of at most 0.0001.
Values sent between devices are 32-bit elements; how exact they have to be, the bound alone decides.
A program may use at most 64 MiB of HBM per device.

v0:
```python
import jax
import jax.numpy as jnp
from jax import lax
from jax.sharding import PartitionSpec as P

PANELS = 4


def contract(rows, weights):
    return lax.dot_general(
        rows,
        weights,
        (((1,), (1,)), ((), ())),
        precision=lax.Precision.HIGHEST,
        preferred_element_type=jnp.float32,
    )


def per_device(amplitudes, integrals):
    n_row = lax.axis_size("row")
    n_col = lax.axis_size("col")
    local_rows = amplitudes.shape[0]
    all_rows = local_rows * n_row * n_col
    total = jnp.zeros((all_rows, integrals.shape[0]), jnp.float32)
    for panel in range(PANELS):
        piece = amplitudes[:, panel, :]
        weights = integrals[:, panel, :]
        regrouped = lax.all_to_all(piece, "col", split_axis=1, concat_axis=0, tiled=True)
        total = total + contract(lax.all_gather(regrouped, "row", axis=0, tiled=True), weights)
    return lax.psum_scatter(total, "col", scatter_dimension=0, tiled=True)


def solution(mesh):
    in_specs = (P(("row", "col"), None, None), P("row", None, "col"))
    out_specs = P("col", "row")
    return jax.shard_map(
        per_device, mesh=mesh, in_specs=in_specs, out_specs=out_specs, check_vma=False
    )
```

profile of v0, /device:TPU:7, one launch (start us, length us, event | category | flops | bytes accessed | tf_op | source)
XLA Modules:
  0.0 483.9 jit_solution(3197056773741636240)
XLA Ops:
  6.5 0.0 all-gather.5.cloned.1.call-start
  6.5 14.5 %slice_reduce_fusion = (f32[96,2048]{1,0:T(8,128)S(1)}, f32[96,2048]{1,0:T(8,128)S(1)}, f32[96,2048]{1,0:T(8,128)S(1)}, f32[96,2048]{1,0:T(8,128)S(1)}) fusion(f32[96,4,2048]{2,1,0:T(4,128)} %param.2), kind=kLoop, calls=%fused_computation.7 | loop fusion | bytes 6291456 | tf_op jit(solution)/shard_map/slice | solution.py:26
  21.0 0.1 copy.42
  21.1 13.7 %all_to_all.76 = f32[96,4,512]{2,0,1:T(8,128)} all-to-all(f32[96,4,512]{2,0,1:T(8,128)S(1)} %bitcast.52), channel_id=1, replica_groups=mesh['row'=8,'col'=4] {'col'}, dimensions={1} | all-to-all | bytes 1572864 | tf_op jit(solution)/shard_map/all_to_all | solution.py:28
  34.7 0.0 all-gather.5.cloned.1.call-update
  34.8 0.0 all-gather.7.cloned.1.call-start
  34.8 0.1 copy.41
  34.9 14.8 %all_to_all.77 = f32[96,4,512]{2,0,1:T(8,128)} all-to-all(f32[96,4,512]{2,0,1:T(8,128)S(1)} %bitcast.53), channel_id=1, replica_groups=mesh['row'=8,'col'=4] {'col'}, dimensions={1} | all-to-all | bytes 1572864 | tf_op jit(solution)/shard_map/all_to_all | solution.py:28
  49.7 0.0 all-gather.7.cloned.1.call-update
  49.7 0.0 all-gather.9.cloned.1.call-start
  49.7 0.1 copy.40
  49.8 0.0 copy-start
  49.8 14.9 %all_to_all.78 = f32[96,4,512]{2,0,1:T(8,128)} all-to-all(f32[96,4,512]{2,0,1:T(8,128)S(1)} %bitcast.54), channel_id=1, replica_groups=mesh['row'=8,'col'=4] {'col'}, dimensions={1} | all-to-all | bytes 1572864 | tf_op jit(solution)/shard_map/all_to_all | solution.py:28
  64.7 0.0 all-gather.9.cloned.1.call-update
  64.8 0.0 all-gather.11.cloned.1.call-start
  64.8 0.1 copy.39
  64.9 14.8 %all_to_all.79 = f32[96,4,512]{2,0,1:T(8,128)} all-to-all(f32[96,4,512]{2,0,1:T(8,128)S(1)} %bitcast.55), channel_id=1, replica_groups=mesh['row'=8,'col'=4] {'col'}, dimensions={1} | all-to-all | bytes 1572864 | tf_op jit(solution)/shard_map/all_to_all | solution.py:28
  79.6 0.0 all-gather.11.cloned.1.call-update
  79.7 0.0 reduce-scatter.2.cloned.1.call-start
  79.7 0.0 copy-done
  79.7 2.8 fusion.1
  82.5 51.3 %all-gather.5.cloned.1.call-done = f32[3072,512]{1,0:T(8,128)} async-done(((f32[384,512]{1,0:T(8,128)}), f32[3072,512]{1,0:T(8,128)}) %all-gather.5.cloned.1.call-update) | async-done | bytes 6291472 | tf_op jit(solution)/shard_map/all_gather | solution.py:29
  133.9 7.3 %fusion = f32[3072,256]{1,0:T(8,128)S(1)} fusion(f32[3072,512]{1,0:T(8,128)} %all-gather.5.cloned.1.call-done, f32[256,1,512]{2,1,0:T(1,128)} %get-tuple-element.12), kind=kOutput, calls=%fused_computation.15 | convolution fusion | flops 4831838208 | bytes 9961472 | tf_op jit(solution)/shard_map/dot_general | solution.py:10
  141.2 92.1 %all-gather.7.cloned.1.call-done = f32[3072,512]{1,0:T(8,128)} async-done(((f32[384,512]{1,0:T(8,128)}), f32[3072,512]{1,0:T(8,128)}) %all-gather.7.cloned.1.call-update) | async-done | bytes 6291472 | tf_op jit(solution)/shard_map/all_gather | solution.py:29
  233.3 8.5 %convolution_add_fusion.2 = f32[3072,256]{1,0:T(8,128)} fusion(f32[3072,256]{1,0:T(8,128)S(1)} %fusion, f32[3072,512]{1,0:T(8,128)} %all-gather.7.cloned.1.call-done, f32[256,1,512]{2,1,0:T(1,128)} %get-tuple-element.11), kind=kOutput, calls=%fused_computation.2 | convolution fusion | flops 4832624640 | bytes 13107200 | tf_op jit(solution)/shard_map/dot_general | solution.py:10
  241.7 91.0 %all-gather.9.cloned.1.call-done = f32[3072,512]{1,0:T(8,128)} async-done(((f32[384,512]{1,0:T(8,128)}), f32[3072,512]{1,0:T(8,128)}) %all-gather.9.cloned.1.call-update) | async-done | bytes 6291472 | tf_op jit(solution)/shard_map/all_gather | solution.py:29
  332.7 7.8 %convolution_add_fusion.1 = f32[3072,256]{1,0:T(8,128)S(1)} fusion(f32[3072,256]{1,0:T(8,128)} %convolution_add_fusion.2, f32[3072,512]{1,0:T(8,128)} %all-gather.9.cloned.1.call-done, f32[256,1,512]{2,1,0:T(1,128)} %get-tuple-element.10), kind=kOutput, calls=%fused_computation.1 | convolution fusion | flops 4832624640 | bytes 13107200 | tf_op jit(solution)/shard_map/dot_general | solution.py:10
  340.5 91.5 %all-gather.11.cloned.1.call-done = f32[3072,512]{1,0:T(8,128)} async-done(((f32[384,512]{1,0:T(8,128)}), f32[3072,512]{1,0:T(8,128)}) %all-gather.11.cloned.1.call-update) | async-done | bytes 6291472 | tf_op jit(solution)/shard_map/all_gather | solution.py:29
  432.0 8.5 %convolution_add_fusion = f32[3072,256]{1,0:T(8,128)} fusion(f32[3072,256]{1,0:T(8,128)S(1)} %convolution_add_fusion.1, f32[3072,512]{1,0:T(8,128)} %all-gather.11.cloned.1.call-done, f32[256,1,512]{2,1,0:T(1,128)} %get-tuple-element.9), kind=kOutput, calls=%fused_computation | convolution fusion | flops 4832624640 | bytes 13107200 | tf_op jit(solution)/shard_map/dot_general | solution.py:10
  440.5 0.0 reduce-scatter.2.cloned.1.call-update
  440.5 36.8 %reduce-scatter.2.cloned.1.call-done = f32[768,256]{1,0:T(8,128)} async-done(((f32[3072,256]{1,0:T(8,128)}), f32[768,256]{1,0:T(8,128)}) %reduce-scatter.2.cloned.1.call-update) | async-done | bytes 786448 | tf_op jit(solution)/shard_map/reduce_scatter | solution.py:30
Async XLA Ops:
  6.5 127.3 %all-gather.5.cloned.1.call-start = ((), (), s32[]{:S(2)}) async-start(), calls=%async_computation.5 | async-start | bytes 7077888 | tf_op jit(solution)/shard_map/all_gather | solution.py:29
  34.8 198.5 %all-gather.7.cloned.1.call-start = ((), (), s32[]{:S(2)}) async-start(), calls=%async_computation.6 | async-start | bytes 7077888 | tf_op jit(solution)/shard_map/all_gather | solution.py:29
  49.7 283.0 %all-gather.9.cloned.1.call-start = ((), (), s32[]{:S(2)}) async-start(), calls=%async_computation.7 | async-start | bytes 7077888 | tf_op jit(solution)/shard_map/all_gather | solution.py:29
  49.8 29.9 %copy-start = (f32[256,4,512]{2,1,0:T(4,128)S(1)}, f32[256,4,512]{2,1,0:T(4,128)}, u32[]{:S(2)}) copy-start(f32[256,4,512]{2,1,0:T(4,128)} %param.3) | copy-start | bytes 6291460
  64.8 367.2 %all-gather.11.cloned.1.call-start = ((), (), s32[]{:S(2)}) async-start(), calls=%async_computation.8 | async-start | bytes 7077888 | tf_op jit(solution)/shard_map/all_gather | solution.py:29
  79.7 397.7 %reduce-scatter.2.cloned.1.call-start = ((), (), s32[]{:S(2)}) async-start(), calls=%async_computation.9 | async-start | bytes 3932160 | tf_op jit(solution)/shard_map/reduce_scatter | solution.py:30
Sparse Core Ops, SparseCore 0:
  34.9 98.9 all-gather.4
  136.0 97.1 all-gather.6
  235.5 97.1 all-gather.8
  334.7 97.1 all-gather.10
  440.7 36.6 reduce-scatter.1
where the time goes:
time: 487 us; the launch traced here: 484 us
  waiting for transfers between devices  363 us (75%)
  blocking collectives  58.1 us (12%)
  matrix products  32.1 us (7%)
  local copies, waits for them, and re-layouts  17.5 us (4%)
  between operations  13.2 us (3%)
    all_gather x4, waiting for transfers between devices, per_device(): lax.all_gather(regrouped, 'row', axis=0, tiled=True)  326 us
    all_to_all x4, blocking collectives, per_device(): lax.all_to_all(piece, 'col', split_axis=1, concat_axis=0, tiled=True)  58.1 us
    reduce_scatter x1, waiting for transfers between devices, per_device(): return lax.psum_scatter(total, 'col', scatter_dimension=0, tiled=True)  36.8 us
    dot_general x4, matrix products, contract(): lax.dot_general(rows, weights, (((1,), (1,)), ((), ())), precision=lax.Pr...  32.1 us
    slice x1, local copies, waits for them, and re-layouts, per_device(): piece = amplitudes[:, panel, :]  14.5 us
  transfers between devices with their start and end apart: 5, of which 5 were waited for; matrix products, arithmetic and copies ran while one was open for 5% of the time, Pallas kernels for 0%

commit v1 on v0

v1 whole, which is shorter than its diff:
```python
import functools

import jax
import jax.numpy as jnp
from jax import lax
from jax.experimental import pallas as pl
from jax.experimental.pallas import tpu as pltpu
from jax.sharding import PartitionSpec as P

MESH = pl.DeviceIdType.MESH
WIDE = 256


def tile_of(extent, most):
    tile = most
    while extent % tile:
        tile //= 2
    return tile


def halves(x):
    high = x.astype(jnp.bfloat16)
    return high, (x - high.astype(jnp.float32)).astype(jnp.bfloat16)


def product(a, b):
    return lax.dot_general(a, b, (((1,), (1,)), ((), ())), preferred_element_type=jnp.float32)


def kernel(
    n_hi, n_lo, a_ref, v_ref, out_ref,
    a_all, v_all, a_high, a_low, v_high, v_low, partial, landed, final,
    own_sem, a_send, a_recv, v_send, v_recv, p_send, p_recv, f_sem,
):
    n_col = n_hi
    row = lax.axis_index("row")
    c = lax.axis_index("col")
    h = lax.div(row, n_lo)
    l = lax.rem(row, n_lo)
    w, panels, _ = a_ref.shape
    nb, _, kc = v_ref.shape
    rows = a_all.shape[0]
    kq = tile_of(kc, WIDE)
    n_chunk = kc // kq
    has = (h > 0, h < n_hi - 1)
    side_of = (-1, 1)

    barrier = pltpu.get_barrier_semaphore()

    def greet(device):
        pl.semaphore_signal(barrier, inc=1, device_id=device, device_id_type=MESH)

    offsets = [(dl, dc) for dl in range(n_lo) for dc in range(n_col) if (dl, dc) != (0, 0)]

    def peer(dl, dc):
        return h * n_lo + lax.rem(l + dl, n_lo), lax.rem(c + dc, n_col)

    for dl, dc in offsets:
        greet(peer(dl, dc))
    for side in range(2):
        @pl.when(has[side])
        def _():
            greet((row + side_of[side] * n_lo, c))

    @pl.when(c != h)
    def _():
        greet((c * n_lo + l, h))

    others = [jnp.where(condition, 1, 0) for condition in (*has, c != h)]
    pl.semaphore_wait(barrier, len(offsets) + sum(others))

    def v_copy(side, d, q):
        s = h - side_of[side] * d
        cols = pl.ds(q * kq, kq)
        source = v_ref.at[:, :, cols] if d == 0 else v_all.at[s, :, :, cols]
        return pltpu.make_async_remote_copy(
            src_ref=source,
            dst_ref=v_all.at[s, :, :, cols],
            send_sem=v_send.at[side, d, q],
            recv_sem=v_recv.at[side, d, q],
            device_id=(row + side_of[side] * n_lo, c),
            device_id_type=MESH,
        )

    def sends(side, d):
        s = h - side_of[side] * d
        return has[side] & (s >= 0) & (s < n_hi)

    def hears(side, d):
        s = h - side_of[side] * d
        return (s >= 0) & (s < n_hi)

    for q in range(n_chunk):
        for side in range(2):
            @pl.when(sends(side, 0))
            def _():
                v_copy(side, 0, q).start()

    def a_copy(dl, dc):
        to_row, to_col = peer(dl, dc)
        return pltpu.make_async_remote_copy(
            src_ref=a_ref.at[:, :, pl.ds(pl.multiple_of(to_col * kc, kc), kc)],
            dst_ref=a_all.at[pl.ds((l * n_col + c) * w, w)],
            send_sem=a_send.at[dl, dc],
            recv_sem=a_recv.at[dl, dc],
            device_id=(to_row, to_col),
            device_id_type=MESH,
        )

    for dl, dc in offsets:
        a_copy(dl, dc).start()
    own_v = pltpu.make_async_copy(v_ref, v_all.at[h], own_sem.at[0])
    own_v.start()
    own_a = pltpu.make_async_copy(
        a_ref.at[:, :, pl.ds(pl.multiple_of(c * kc, kc), kc)], a_all.at[pl.ds((l * n_col + c) * w, w)], own_sem.at[1]
    )
    own_a.start()

    def forward(d, q):
        for side in range(2):
            @pl.when(hears(side, d))
            def _():
                s = h - side_of[side] * d
                cols = pl.ds(q * kq, kq)
                pltpu.make_async_remote_copy(
                    src_ref=v_all.at[s, :, :, cols],
                    dst_ref=v_all.at[s, :, :, cols],
                    send_sem=v_send.at[side, d - 1, q],
                    recv_sem=v_recv.at[side, d - 1, q],
                    device_id=(row, c),
                    device_id_type=MESH,
                ).wait_recv()
                if d < n_hi - 1:
                    @pl.when(has[side])
                    def _():
                        v_copy(side, d, q).start()

    def take_a():
        own_a.wait()
        for dl, dc in offsets:
            from_l, from_c = lax.rem(l + n_lo - dl, n_lo), lax.rem(c + n_col - dc, n_col)
            pltpu.make_async_remote_copy(
                src_ref=a_all.at[pl.ds((from_l * n_col + from_c) * w, w)],
                dst_ref=a_all.at[pl.ds((from_l * n_col + from_c) * w, w)],
                send_sem=a_send.at[dl, dc],
                recv_sem=a_recv.at[dl, dc],
                device_id=(row, c),
                device_id_type=MESH,
            ).wait_recv()
        t = tile_of(rows, 32)

        @pl.loop(0, rows // t)
        def _(i):
            at = pl.ds(pl.multiple_of(i * t, t), t)
            for p in range(panels):
                a_high[at, pl.ds(p * kc, kc)], a_low[at, pl.ds(p * kc, kc)] = halves(a_all[at, p, :])

    def multiply(s, q):
        t = tile_of(nb, 32)

        @pl.loop(0, nb // t)
        def _(i):
            at = pl.ds(pl.multiple_of(i * t, t), t)
            for p in range(panels):
                v_high[at, pl.ds(p * kq, kq)], v_low[at, pl.ds(p * kq, kq)] = halves(
                    v_all[s, at, p, pl.ds(q * kq, kq)]
                )

        m = tile_of(rows, 256)

        @pl.loop(0, rows // m)
        def _(i):
            at = pl.ds(pl.multiple_of(i * m, m), m)
            total = None if q == 0 else partial[s, at, :]
            for p in range(panels):
                a_cols, v_cols = pl.ds(p * kc + q * kq, kq), pl.ds(p * kq, kq)
                ah, al = a_high[at, a_cols], a_low[at, a_cols]
                vh, vl = v_high[:, v_cols], v_low[:, v_cols]
                term = product(ah, vh) + (product(ah, vl) + product(al, vh))
                total = term if total is None else total + term
            partial[s, at, :] = total

    def p_copy(s, k):
        return pltpu.make_async_remote_copy(
            src_ref=partial.at[s],
            dst_ref=landed.at[c],
            send_sem=p_send.at[k],
            recv_sem=p_recv.at[c],
            device_id=(row, s),
            device_id_type=MESH,
        )

    def blocks(d):
        if d == 0:
            return [(0, None, h)]
        return [(2 * d - 1 + side, hears(side, d), h - side_of[side] * d) for side in range(2)]

    def compute(d, q):
        for k, condition, s in blocks(d):
            def run():
                multiply(s, q)
                if q == n_chunk - 1:
                    @pl.when(s != c)
                    def _():
                        p_copy(s, k).start()
            run() if condition is None else pl.when(condition)(run)

    chunks = range(n_chunk)
    for q in chunks:
        forward(1, q)
    take_a()
    own_v.wait()
    for q in chunks:
        compute(0, q)
    if n_hi > 2:
        forward(2, 0)
    for q in chunks:
        compute(1, q)
    for d in range(2, n_hi):
        for q in chunks:
            if (d, q) != (2, 0):
                forward(d, q)
            compute(d, q)

    for dc in range(1, n_col):
        from_c = lax.rem(c + dc, n_col)
        pltpu.make_async_remote_copy(
            src_ref=landed.at[from_c],
            dst_ref=landed.at[from_c],
            send_sem=p_send.at[0],
            recv_sem=p_recv.at[from_c],
            device_id=(row, c),
            device_id_type=MESH,
        ).wait_recv()
    t = tile_of(rows, 64)

    @pl.loop(0, rows // t)
    def _(i):
        at = pl.ds(pl.multiple_of(i * t, t), t)
        total = partial[c, at, :]
        for dc in range(1, n_col):
            total = total + landed[lax.rem(c + dc, n_col), at, :]
        final[at, :] = total

    @pl.when(c != h)
    def _():
        copy = pltpu.make_async_remote_copy(
            src_ref=final,
            dst_ref=out_ref,
            send_sem=f_sem.at[0],
            recv_sem=f_sem.at[1],
            device_id=(c * n_lo + l, h),
            device_id_type=MESH,
        )
        copy.start()
        copy.wait()

    @pl.when(c == h)
    def _():
        copy = pltpu.make_async_copy(final, out_ref, f_sem.at[0])
        copy.start()
        copy.wait()

    for dl, dc in offsets:
        a_copy(dl, dc).wait_send()
    for side in range(2):
        for d in range(n_hi - 1):
            @pl.when(sends(side, d))
            def _():
                for q in chunks:
                    v_copy(side, d, q).wait_send()
    for d in range(n_hi):
        for k, condition, s in blocks(d):
            there = s != c if condition is None else condition & (s != c)

            @pl.when(there)
            def _():
                p_copy(s, k).wait_send()


def per_device(amplitudes, integrals):
    n_row = lax.axis_size("row")
    n_col = lax.axis_size("col")
    n_lo = n_row // n_col
    w, panels, _ = amplitudes.shape
    nb, _, kc = integrals.shape
    rows = w * n_lo * n_col
    kq = tile_of(kc, WIDE)
    n_chunk = kc // kq
    f32, bf16 = jnp.float32, jnp.bfloat16
    dma = pltpu.SemaphoreType.DMA
    return pl.pallas_call(
        functools.partial(kernel, n_col, n_lo),
        out_shape=jax.ShapeDtypeStruct((rows, nb), f32),
        in_specs=[pl.BlockSpec(memory_space=pl.ANY)] * 2,
        out_specs=pl.BlockSpec(memory_space=pl.ANY),
        scratch_shapes=[
            pltpu.VMEM((rows, panels, kc), f32),
            pltpu.VMEM((n_col, nb, panels, kc), f32),
            pltpu.VMEM((rows, panels * kc), bf16),
            pltpu.VMEM((rows, panels * kc), bf16),
            pltpu.VMEM((nb, panels * kq), bf16),
            pltpu.VMEM((nb, panels * kq), bf16),
            pltpu.VMEM((n_col, rows, nb), f32),
            pltpu.VMEM((n_col, rows, nb), f32),
            pltpu.VMEM((rows, nb), f32),
            dma((2,)),
            dma((n_lo, n_col)),
            dma((n_lo, n_col)),
            dma((2, n_col, n_chunk)),
            dma((2, n_col, n_chunk)),
            dma((2 * n_col,)),
            dma((n_col,)),
            dma((2,)),
        ],
        compiler_params=pltpu.CompilerParams(
            collective_id=0, has_side_effects=True, vmem_limit_bytes=48 * 2**20
        ),
        cost_estimate=pl.CostEstimate(
            flops=6 * rows * nb * n_col * panels * kc, bytes_accessed=4 * (amplitudes.size + integrals.size), transcendentals=0
        ),
    )(amplitudes, integrals)


def solution(mesh):
    in_specs = (P(("row", "col"), None, None), P("row", None, "col"))
    out_specs = P("col", "row")
    return jax.shard_map(
        per_device, mesh=mesh, in_specs=in_specs, out_specs=out_specs, check_vma=False
    )
```

time: 487 us -> 208 us (0.43)
  waiting for transfers between devices: 363 us -> 0 us
  Pallas kernels: 0 us -> 204 us
  blocking collectives: 58.1 us -> 0 us
  matrix products: 32.1 us -> 0 us
  between operations: 13.2 us -> 0.01 us
  local copies, waits for them, and re-layouts: 17.5 us -> 4.36 us
    all_gather x4 -> x0, waiting for transfers between devices: 326 us -> none  [per_device(): lax.all_gather(regrouped, 'row', axis=0, tiled=True)]
    pallas_call x0 -> x1, Pallas kernels: none -> 204 us  [per_device(): pl.pallas_call(functools.partial(kernel, n_col, n_lo), out_shape=jax.Shap...]
    all_to_all x4 -> x0, blocking collectives: 58.1 us -> none  [per_device(): lax.all_to_all(piece, 'col', split_axis=1, concat_axis=0, tiled=True)]
    reduce_scatter x1 -> x0, waiting for transfers between devices: 36.8 us -> none  [per_device(): return lax.psum_scatter(total, 'col', scatter_dimension=0, tiled=True)]
    dot_general x4 -> x0, matrix products: 32.1 us -> none  [contract(): lax.dot_general(rows, weights, (((1,), (1,)), ((), ())), precision=lax.Pr...]
    slice x2 -> x0, local copies, waits for them, and re-layouts: 17.2 us -> none  [the longest x1 14.5 us: per_device(): piece = amplitudes[:, panel, :]]
  transfers between devices with their start and end apart: 5 -> 0, of which waited for: 5 -> 0; matrix products, arithmetic and copies ran while one was open for 5% -> 0% of each run, Pallas kernels for 0% -> 0%
where the time goes in v1:
time: 208 us
  Pallas kernels  204 us (98%)
  local copies, waits for them, and re-layouts  4.36 us (2%)
    pallas_call x1, Pallas kernels, per_device(): pl.pallas_call(functools.partial(kernel, n_col, n_lo), out_shape=jax.Shap...  204 us
    unnamed x5, local copies, waits for them, and re-layouts  4.36 us

profile of v1, /device:TPU:7, one launch (start us, length us, event | category | flops | bytes accessed | tf_op | source)
XLA Modules:
  0.0 208.1 jit_solution(9800889047062409368)
XLA Ops:
  0.0 0.0 copy-start
  0.0 1.9 copy-done
  1.9 0.0 copy-start.1
  1.9 1.6 copy-done.1
  3.5 203.7 %shard_map.28 = f32[768,256]{1,0:T(8,128)S(1)} custom-call(f32[96,4,2048]{2,1,0:T(4,128)S(1)} %copy-done, f32[256,4,512]{2,1,0:T(4,128)S(1)} %copy-done.1), custom_call_target="tpu_custom_call" | custom-call | flops 9663676416 | bytes 5242880 | tf_op jit(solution)/shard_map/pallas_call | solution.py:292
  207.2 0.9 copy.4
Async XLA Ops:
  0.0 1.9 copy-start
  1.9 1.6 copy-start.1

commit v2 on v1

--- a/solution.py
+++ b/solution.py
@@ -208,17 +208,18 @@
     chunks = range(n_chunk)
     for q in chunks:
         forward(1, q)
+    if n_hi > 2:
+        forward(2, 0)
     take_a()
     own_v.wait()
     for q in chunks:
         compute(0, q)
     if n_hi > 2:
-        forward(2, 0)
-    for q in chunks:
-        compute(1, q)
-    for d in range(2, n_hi):
+        for q in chunks[1:]:
+            forward(2, q)
+    for d in range(1, n_hi):
         for q in chunks:
-            if (d, q) != (2, 0):
+            if d > 2:
                 forward(d, q)
             compute(d, q)
 
@@ -232,34 +233,44 @@
             device_id=(row, c),
             device_id_type=MESH,
         ).wait_recv()
-    t = tile_of(rows, 64)
-
-    @pl.loop(0, rows // t)
-    def _(i):
-        at = pl.ds(pl.multiple_of(i * t, t), t)
-        total = partial[c, at, :]
-        for dc in range(1, n_col):
-            total = total + landed[lax.rem(c + dc, n_col), at, :]
-        final[at, :] = total
-
-    @pl.when(c != h)
-    def _():
-        copy = pltpu.make_async_remote_copy(
-            src_ref=final,
-            dst_ref=out_ref,
-            send_sem=f_sem.at[0],
-            recv_sem=f_sem.at[1],
+    n_piece = f_sem.shape[1]
+    step = rows // n_piece
+    t = tile_of(step, 64)
+
+    def far(k):
+        part = pl.ds(k * step, step)
+        return pltpu.make_async_remote_copy(
+            src_ref=final.at[part],
+            dst_ref=out_ref.at[part],
+            send_sem=f_sem.at[0, k],
+            recv_sem=f_sem.at[1, k],
             device_id=(c * n_lo + l, h),
             device_id_type=MESH,
         )
-        copy.start()
-        copy.wait()
-
-    @pl.when(c == h)
-    def _():
-        copy = pltpu.make_async_copy(final, out_ref, f_sem.at[0])
-        copy.start()
-        copy.wait()
+
+    def near(k):
+        part = pl.ds(k * step, step)
+        return pltpu.make_async_copy(final.at[part], out_ref.at[part], f_sem.at[0, k])
+
+    for k in range(n_piece):
+        @pl.loop(0, step // t)
+        def _(i):
+            at = pl.ds(pl.multiple_of(k * step + i * t, t), t)
+            total = partial[c, at, :]
+            for dc in range(1, n_col):
+                total = total + landed[lax.rem(c + dc, n_col), at, :]
+            final[at, :] = total
+
+        for there, copy in ((c != h, far), (c == h, near)):
+            @pl.when(there)
+            def _():
+                copy(k).start()
+
+    for there, copy in ((c != h, far), (c == h, near)):
+        @pl.when(there)
+        def _():
+            for k in range(n_piece):
+                copy(k).wait()
 
     for dl, dc in offsets:
         a_copy(dl, dc).wait_send()
@@ -311,7 +322,7 @@
             dma((2, n_col, n_chunk)),
             dma((2 * n_col,)),
             dma((n_col,)),
-            dma((2,)),
+            dma((2, tile_of(rows // 8, 4))),
         ],
         compiler_params=pltpu.CompilerParams(
             collective_id=0, has_side_effects=True, vmem_limit_bytes=48 * 2**20

time: 208 us -> 199 us (0.957)
  Pallas kernels: 204 us -> 193 us
    pallas_call x1, Pallas kernels: 204 us -> 193 us  [per_device(): pl.pallas_call(functools.partial(kernel, n_col, n_lo), out_shape=jax.Shap...]
where the time goes in v2:
time: 199 us; the launch traced here: 197 us
  Pallas kernels  193 us (97%)
  local copies, waits for them, and re-layouts  4.36 us (2%)
    pallas_call x1, Pallas kernels, per_device(): pl.pallas_call(functools.partial(kernel, n_col, n_lo), out_shape=jax.Shap...  193 us
    unnamed x5, local copies, waits for them, and re-layouts  4.36 us

profile of v2, /device:TPU:7, one launch (start us, length us, event | category | flops | bytes accessed | tf_op | source)
XLA Modules:
  0.0 197.3 jit_solution(16487812790574185900)
XLA Ops:
  0.0 0.0 copy-start
  0.0 1.9 copy-done
  1.9 0.0 copy-start.1
  1.9 1.6 copy-done.1
  3.5 192.9 %shard_map.28 = f32[768,256]{1,0:T(8,128)S(1)} custom-call(f32[96,4,2048]{2,1,0:T(4,128)S(1)} %copy-done, f32[256,4,512]{2,1,0:T(4,128)S(1)} %copy-done.1), custom_call_target="tpu_custom_call" | custom-call | flops 9663676416 | bytes 5242880 | tf_op jit(solution)/shard_map/pallas_call | solution.py:303
  196.4 0.9 copy.4
Async XLA Ops:
  0.0 1.9 copy-start
  1.9 1.6 copy-start.1

commit v3 on v2

--- a/solution.py
+++ b/solution.py
@@ -23,6 +23,11 @@
     return high, (x - high.astype(jnp.float32)).astype(jnp.bfloat16)
 
 
+def rows_at_once(extent, most):
+    tile = tile_of(extent, most)
+    return extent if tile % 16 else tile
+
+
 def product(a, b):
     return lax.dot_general(a, b, (((1,), (1,)), ((), ())), preferred_element_type=jnp.float32)
 
@@ -30,7 +35,7 @@
 def kernel(
     n_hi, n_lo, a_ref, v_ref, out_ref,
     a_all, v_all, a_high, a_low, v_high, v_low, partial, landed, final,
-    own_sem, a_send, a_recv, v_send, v_recv, p_send, p_recv, f_sem,
+    own_sem, a_send, a_recv, v_send, v_recv, p_send, p_recv, f_send, f_recv,
 ):
     n_col = n_hi
     row = lax.axis_index("row")
@@ -39,7 +44,7 @@
     l = lax.rem(row, n_lo)
     w, panels, _ = a_ref.shape
     nb, _, kc = v_ref.shape
-    rows = a_all.shape[0]
+    step = partial.shape[2]
     kq = tile_of(kc, WIDE)
     n_chunk = kc // kq
     has = (h > 0, h < n_hi - 1)
@@ -62,12 +67,15 @@
         def _():
             greet((row + side_of[side] * n_lo, c))
 
-    @pl.when(c != h)
-    def _():
-        greet((c * n_lo + l, h))
-
+    def is_self(to_h, to_c):
+        return (to_h == h) & (to_c == c)
+
+    for j in range(n_col):
+        @pl.when(jnp.logical_not(is_self(c, j)))
+        def _():
+            greet((c * n_lo + l, j))
     others = [jnp.where(condition, 1, 0) for condition in (*has, c != h)]
-    pl.semaphore_wait(barrier, len(offsets) + sum(others))
+    pl.semaphore_wait(barrier, len(offsets) + n_hi - 1 + sum(others))
 
     def v_copy(side, d, q):
         s = h - side_of[side] * d
@@ -147,13 +155,16 @@
                 device_id=(row, c),
                 device_id_type=MESH,
             ).wait_recv()
-        t = tile_of(rows, 32)
-
-        @pl.loop(0, rows // t)
+        t = rows_at_once(step, 32)
+
+        @pl.loop(0, n_col)
         def _(i):
-            at = pl.ds(pl.multiple_of(i * t, t), t)
-            for p in range(panels):
-                a_high[at, pl.ds(p * kc, kc)], a_low[at, pl.ds(p * kc, kc)] = halves(a_all[at, p, :])
+            @pl.loop(0, step // t)
+            def _(j):
+                at = pl.ds(0, t) if t == step else pl.ds(pl.multiple_of(j * t, t), t)
+                for p in range(panels):
+                    cols = pl.ds(p * kc, kc)
+                    a_high[i, at, cols], a_low[i, at, cols] = halves(a_all[pl.ds(i * step + j * t, t), p, :])
 
     def multiply(s, q):
         t = tile_of(nb, 32)
@@ -166,29 +177,40 @@
                     v_all[s, at, p, pl.ds(q * kq, kq)]
                 )
 
-        m = tile_of(rows, 256)
-
-        @pl.loop(0, rows // m)
+        @pl.loop(0, n_col)
         def _(i):
-            at = pl.ds(pl.multiple_of(i * m, m), m)
-            total = None if q == 0 else partial[s, at, :]
+            total = None if q == 0 else partial[s, i]
             for p in range(panels):
                 a_cols, v_cols = pl.ds(p * kc + q * kq, kq), pl.ds(p * kq, kq)
-                ah, al = a_high[at, a_cols], a_low[at, a_cols]
+                ah, al = a_high[i, :, a_cols], a_low[i, :, a_cols]
                 vh, vl = v_high[:, v_cols], v_low[:, v_cols]
                 term = product(ah, vh) + (product(ah, vl) + product(al, vh))
                 total = term if total is None else total + term
-            partial[s, at, :] = total
-
-    def p_copy(s, k):
+            partial[s, i] = total
+
+    def p_copy(s, k, dc):
+        to_c = lax.rem(c + dc, n_col)
         return pltpu.make_async_remote_copy(
-            src_ref=partial.at[s],
-            dst_ref=landed.at[c],
-            send_sem=p_send.at[k],
-            recv_sem=p_recv.at[c],
-            device_id=(row, s),
+            src_ref=partial.at[s, to_c],
+            dst_ref=landed.at[s, c],
+            send_sem=p_send.at[k, dc],
+            recv_sem=p_recv.at[k, dc],
+            device_id=(row, to_c),
             device_id_type=MESH,
         )
+
+    def f_copy(s, k):
+        return pltpu.make_async_remote_copy(
+            src_ref=final.at[s],
+            dst_ref=out_ref.at[c],
+            send_sem=f_send.at[k],
+            recv_sem=f_recv.at[c],
+            device_id=(s * n_lo + l, h),
+            device_id_type=MESH,
+        )
+
+    def f_near():
+        return pltpu.make_async_copy(final.at[h], out_ref.at[c], own_sem.at[2])
 
     def blocks(d):
         if d == 0:
@@ -200,9 +222,38 @@
             def run():
                 multiply(s, q)
                 if q == n_chunk - 1:
-                    @pl.when(s != c)
-                    def _():
-                        p_copy(s, k).start()
+                    for dc in range(1, n_col):
+                        p_copy(s, k, dc).start()
+            run() if condition is None else pl.when(condition)(run)
+
+    def finish(d):
+        for k, condition, s in blocks(d):
+            def run():
+                for dc in range(1, n_col):
+                    from_c = lax.rem(c + n_col - dc, n_col)
+                    pltpu.make_async_remote_copy(
+                        src_ref=landed.at[s, from_c],
+                        dst_ref=landed.at[s, from_c],
+                        send_sem=p_send.at[k, dc],
+                        recv_sem=p_recv.at[k, dc],
+                        device_id=(row, c),
+                        device_id_type=MESH,
+                    ).wait_recv()
+                t = rows_at_once(step, 64)
+
+                @pl.loop(0, step // t)
+                def _(j):
+                    at = pl.ds(0, t) if t == step else pl.ds(pl.multiple_of(j * t, t), t)
+                    total = partial[s, c, at, :]
+                    for dc in range(1, n_col):
+                        total = total + landed[s, lax.rem(c + dc, n_col), at, :]
+                    final[s, at, :] = total
+
+                if d == 0:
+                    pl.when(c != h)(lambda: f_copy(s, k).start())
+                    pl.when(c == h)(lambda: f_near().start())
+                else:
+                    f_copy(s, k).start()
             run() if condition is None else pl.when(condition)(run)
 
     chunks = range(n_chunk)
@@ -222,55 +273,22 @@
             if d > 2:
                 forward(d, q)
             compute(d, q)
-
-    for dc in range(1, n_col):
-        from_c = lax.rem(c + dc, n_col)
-        pltpu.make_async_remote_copy(
-            src_ref=landed.at[from_c],
-            dst_ref=landed.at[from_c],
-            send_sem=p_send.at[0],
-            recv_sem=p_recv.at[from_c],
-            device_id=(row, c),
-            device_id_type=MESH,
-        ).wait_recv()
-    n_piece = f_sem.shape[1]
-    step = rows // n_piece
-    t = tile_of(step, 64)
-
-    def far(k):
-        part = pl.ds(k * step, step)
-        return pltpu.make_async_remote_copy(
-            src_ref=final.at[part],
-            dst_ref=out_ref.at[part],
-            send_sem=f_sem.at[0, k],
-            recv_sem=f_sem.at[1, k],
-            device_id=(c * n_lo + l, h),
-            device_id_type=MESH,
-        )
-
-    def near(k):
-        part = pl.ds(k * step, step)
-        return pltpu.make_async_copy(final.at[part], out_ref.at[part], f_sem.at[0, k])
-
-    for k in range(n_piece):
-        @pl.loop(0, step // t)
-        def _(i):
-            at = pl.ds(pl.multiple_of(k * step + i * t, t), t)
-            total = partial[c, at, :]
-            for dc in range(1, n_col):
-                total = total + landed[lax.rem(c + dc, n_col), at, :]
-            final[at, :] = total
-
-        for there, copy in ((c != h, far), (c == h, near)):
-            @pl.when(there)
-            def _():
-                copy(k).start()
-
-    for there, copy in ((c != h, far), (c == h, near)):
-        @pl.when(there)
+            if q == 0:
+                finish(d - 1)
+    finish(n_hi - 1)
+
+    for j in range(n_col):
+        @pl.when(jnp.logical_not(is_self(c, j)))
         def _():
-            for k in range(n_piece):
-                copy(k).wait()
+            pltpu.make_async_remote_copy(
+                src_ref=final.at[0],
+                dst_ref=out_ref.at[j],
+                send_sem=f_send.at[0],
+                recv_sem=f_recv.at[j],
+                device_id=(row, c),
+                device_id_type=MESH,
+            ).wait_recv()
+    pl.when(c == h)(lambda: f_near().wait())
 
     for dl, dc in offsets:
         a_copy(dl, dc).wait_send()
@@ -282,11 +300,14 @@
                     v_copy(side, d, q).wait_send()
     for d in range(n_hi):
         for k, condition, s in blocks(d):
-            there = s != c if condition is None else condition & (s != c)
-
-            @pl.when(there)
-            def _():
-                p_copy(s, k).wait_send()
+            def run():
+                for dc in range(1, n_col):
+                    p_copy(s, k, dc).wait_send()
+                if d == 0:
+                    pl.when(c != h)(lambda: f_copy(s, k).wait_send())
+                else:
+                    f_copy(s, k).wait_send()
+            run() if condition is None else pl.when(condition)(run)
 
 
 def per_device(amplitudes, integrals):
@@ -300,29 +321,31 @@
     n_chunk = kc // kq
     f32, bf16 = jnp.float32, jnp.bfloat16
     dma = pltpu.SemaphoreType.DMA
-    return pl.pallas_call(
+    step = rows // n_col
+    ladder = pl.pallas_call(
         functools.partial(kernel, n_col, n_lo),
-        out_shape=jax.ShapeDtypeStruct((rows, nb), f32),
+        out_shape=jax.ShapeDtypeStruct((n_col, step, nb), f32),
         in_specs=[pl.BlockSpec(memory_space=pl.ANY)] * 2,
         out_specs=pl.BlockSpec(memory_space=pl.ANY),
         scratch_shapes=[
             pltpu.VMEM((rows, panels, kc), f32),
             pltpu.VMEM((n_col, nb, panels, kc), f32),
-            pltpu.VMEM((rows, panels * kc), bf16),
-            pltpu.VMEM((rows, panels * kc), bf16),
+            pltpu.VMEM((n_col, step, panels * kc), bf16),
+            pltpu.VMEM((n_col, step, panels * kc), bf16),
             pltpu.VMEM((nb, panels * kq), bf16),
             pltpu.VMEM((nb, panels * kq), bf16),
-            pltpu.VMEM((n_col, rows, nb), f32),
-            pltpu.VMEM((n_col, rows, nb), f32),
-            pltpu.VMEM((rows, nb), f32),
-            dma((2,)),
+            pltpu.VMEM((n_col, n_col, step, nb), f32),
+            pltpu.VMEM((n_col, n_col, step, nb), f32),
+            pltpu.VMEM((n_col, step, nb), f32),
+            dma((3,)),
             dma((n_lo, n_col)),
             dma((n_lo, n_col)),
             dma((2, n_col, n_chunk)),
             dma((2, n_col, n_chunk)),
+            dma((2 * n_col, n_col)),
+            dma((2 * n_col, n_col)),
             dma((2 * n_col,)),
             dma((n_col,)),
-            dma((2, tile_of(rows // 8, 4))),
         ],
         compiler_params=pltpu.CompilerParams(
             collective_id=0, has_side_effects=True, vmem_limit_bytes=48 * 2**20
@@ -331,6 +354,7 @@
             flops=6 * rows * nb * n_col * panels * kc, bytes_accessed=4 * (amplitudes.size + integrals.size), transcendentals=0
         ),
     )(amplitudes, integrals)
+    return ladder.reshape(rows, nb)
 
 
 def solution(mesh):

time: 199 us -> 173 us (0.87)
  the two profiles are of different devices: /device:TPU:7 before, /device:TPU:4 now
where the time goes in v3:
time: 173 us
  Pallas kernels  169 us (98%)
  local copies, waits for them, and re-layouts  4.36 us (3%)
    pallas_call x1, Pallas kernels, per_device(): pl.pallas_call(functools.partial(kernel, n_col, n_lo), out_shape=jax.Shap...  169 us
    unnamed x5, local copies, waits for them, and re-layouts  4.36 us

profile of v3, /device:TPU:4, one launch (start us, length us, event | category | flops | bytes accessed | tf_op | source)
XLA Modules:
  0.0 173.0 jit_solution(1468406295176044606)
XLA Ops:
  0.0 0.0 copy-start
  0.0 1.9 %copy-done = f32[96,4,2048]{2,1,0:T(4,128)S(1)} copy-done((f32[96,4,2048]{2,1,0:T(4,128)S(1)}, f32[96,4,2048]{2,1,0:T(4,128)}, u32[]{:S(2)}) %copy-start) | copy-done | bytes 3145752
  1.9 0.0 copy-start.1
  1.9 1.6 copy-done.1
  3.5 168.6 %shard_map.28 = f32[4,192,256]{2,1,0:T(8,128)S(1)} custom-call(f32[96,4,2048]{2,1,0:T(4,128)S(1)} %copy-done, f32[256,4,512]{2,1,0:T(4,128)S(1)} %copy-done.1), custom_call_target="tpu_custom_call" | custom-call | flops 9663676416 | bytes 5242880 | tf_op jit(solution)/shard_map/pallas_call | solution.py:325
  172.1 0.9 copy.4
Async XLA Ops:
  0.0 1.9 %copy-start = (f32[96,4,2048]{2,1,0:T(4,128)S(1)}, f32[96,4,2048]{2,1,0:T(4,128)}, u32[]{:S(2)}) copy-start(f32[96,4,2048]{2,1,0:T(4,128)} %a_ref.1) | copy-start | bytes 9437188
  1.9 1.6 copy-start.1
